TPU v7x, 512 devices: a whole 4x4x16 slice. The times are simulated.
512 devices in a mesh: sub: 32 (over z, core), blk: 16 (over y, x).
Axes of the slice: x: 4, y: 4, z: 16, core: 2. Of those that a mesh axis runs over, the one named last changes fastest.
Arguments:
- impedance: bfloat16 [32, 16384, 1024], P('sub', 'blk'), may hold values from -0.1875 to 0.1875
- port_node: int32 [32, 1024], P('sub', 'blk'), may hold values from 0 to 16383, as said below
- far_system: int32 [32, 1024], P('sub', 'blk'), may hold values from 0 to 31, as said below
- delays: int32 [32, 1024], P('sub', 'blk'), may hold values from 2 to 4, as said below
- admittance: float32 [32, 1024], P('sub', 'blk'), may hold values from 0.5 to 2
- pole_rates: float32 [32, 12, 1024], P('sub', None, 'blk'), may hold values from 0.05 to 0.95
- residues: float32 [32, 12, 1024], P('sub', None, 'blk'), may hold values from -1.8 to 1.8
- states: float32 [32, 12, 1024, 256], P('sub', None, 'blk'), may hold values from -3 to 3
- history: float32 [32, 4, 1024, 256], P('sub', None, 'blk'), may hold values from -6 to 6
- event_port: int32 [32, 256], P('sub'), may hold values from 0 to 1023
- amplitude: float32 [32, 2, 256], P('sub'), may hold values from -48 to 48
Outputs:
- peak_voltage: bfloat16 [32, 16384, 256], P('sub', 'blk')
- new_states: float32 [32, 12, 1024, 256], P('sub', None, 'blk')
- arrived: float32 [32, 1024, 2, 256], P('sub', 'blk')
Inputs may be any that keep to these rules, and one draw needn't show every extreme that they name: `port_node`: the node of terminal j lies in rows (j // 64) * 1024 to (j // 64 + 1) * 1024 - 1; the terminals of one subsystem have distinct nodes. Line j joins terminal j of two different subsystems: far_system[far_system[s, j], j] = s and far_system[s, j] != s. Of the terminals b * 64 to (b + 1) * 64 - 1 of one subsystem at most 6 lead to one same subsystem, and in every such group exactly 6 do for one of them. delays[s, j] = delays[far_system[s, j], j].
All inputs are finite; a program needn't handle non-finite values.
Results may differ from a plain program's by a relative error of at most 0.0042.
Values may be sent and summed in bfloat16 or wider, within the bound.
A program may use at most 64 MiB of HBM per device.

v0:
```python
import jax
import jax.numpy as jnp
from jax import lax
from jax.sharding import PartitionSpec as P


def pick_incident(history, delays, step_index):
    depth_iota = jnp.arange(history.shape[0], dtype=jnp.int32)
    wanted = delays - step_index - 1
    chosen = jnp.where(wanted[None, :, None] == depth_iota[:, None, None], history, 0.0)
    return jnp.sum(chosen, axis=0)


def deliver(emitted, partners):
    port_count = partners.shape[0]
    columns = emitted.shape[1]
    local_index = jnp.arange(port_count, dtype=jnp.int32)
    earlier = local_index[:, None] > local_index[None, :]
    slot_ranks = jnp.sum(jnp.logical_and(partners[:, None] == partners[None, :], earlier), axis=1)
    systems = lax.axis_size("sub")
    surplus = max(1, port_count // 16)
    capacity = (port_count - surplus + systems - 2) // (systems - 1) + surplus
    slot_rows = partners * capacity + slot_ranks
    outbox = jnp.zeros((systems * capacity, columns), jnp.float32).at[slot_rows].set(emitted)
    received = lax.all_to_all(
        outbox.reshape(systems, capacity, columns), "sub", split_axis=0, concat_axis=0, tiled=True
    )
    return received.reshape(systems * capacity, columns)[slot_rows]


def body(
    impedance,
    port_node,
    far_system,
    delays,
    admittance,
    pole_rates,
    residues,
    states,
    history,
    event_port,
    amplitude,
):
    node_rows = impedance.shape[1]
    port_count = port_node.shape[1]
    scenarios = states.shape[3]
    steps_total = amplitude.shape[1]
    block_index = lax.axis_index("blk")
    port_index = block_index * port_count + jnp.arange(port_count, dtype=jnp.int32)
    local_nodes = port_node[0] - block_index * node_rows
    matrix = impedance[0]
    decay_rates = pole_rates[0][:, :, None]
    weights = residues[0][:, :, None]
    partners = far_system[0]
    line_admittance = admittance[0][:, None]
    current = states[0]
    sources = []
    injections = []
    for step_index in range(steps_total):
        incident = pick_incident(history[0], delays[0], step_index)
        current = decay_rates * current + weights * incident[None]
        source = jnp.sum(current, axis=0)
        switched = jnp.where(
            event_port[0][None, :] == port_index[:, None], amplitude[0, step_index][None, :], 0.0
        )
        sources.append(source)
        injections.append((source + switched).astype(jnp.bfloat16))
    voltages = []
    arrivals = []
    for step_index in range(steps_total):
        voltage = jnp.dot(
            matrix,
            lax.all_gather(injections[step_index], "blk", axis=0, tiled=True),
            preferred_element_type=jnp.float32,
        )
        voltages.append(voltage)
        emitted_now = 2.0 * line_admittance * voltage[local_nodes] - sources[step_index]
        arrivals.append(deliver(emitted_now, partners))
    arrived = jnp.stack(arrivals, axis=1)
    peak_value = jnp.zeros((node_rows, scenarios), jnp.float32)
    for voltage in voltages:
        peak_value = jnp.maximum(peak_value, jnp.abs(voltage))
    return (peak_value.astype(jnp.bfloat16)[None], current[None], arrived[None])


def solution(mesh):
    placed = (
        P("sub", "blk", None),
        P("sub", "blk"),
        P("sub", "blk"),
        P("sub", "blk"),
        P("sub", "blk"),
        P("sub", None, "blk"),
        P("sub", None, "blk"),
        P("sub", None, "blk", None),
        P("sub", None, "blk", None),
        P("sub", None),
        P("sub", None, None),
    )
    return jax.shard_map(
        body,
        mesh=mesh,
        in_specs=placed,
        out_specs=(P("sub", "blk", None), P("sub", None, "blk", None), P("sub", "blk", None, None)),
        check_vma=False,
    )
```

profile of v0, /device:TPU:1, one launch (start us, length us, event | category | flops | bytes accessed | tf_op | source)
XLA Modules:
  0.0 123.7 jit_solution(7459575699059238528)
XLA Ops:
  0.6 0.0 copy-start
  0.6 0.8 add_bitcast_fusion
  1.5 0.8 fusion.34
  2.2 0.7 copy_bitcast_fusion
  2.9 1.1 fusion.13
  4.1 1.4 %fusion.11 = (f32[64,256]{1,0:T(8,128)S(1)}, f32[64,256]{1,0:T(8,128)S(1)}) fusion(f32[1,12,64,256]{3,2,1,0:T(8,128)} %param.18, f32[64,256]{1,0:T(8,128)S(1)} %get-tuple-element.14, f32[12,64]{1,0:T(8,128)S(1)} %get-tuple-element.24, f32[12,64]{1,0:T(8,128)S(1)} %get-tuple-element.25, f32[64,256]{1,0:T(8,128)S(1)} %get-tuple-element.15), kind=kLoop, calls=%fused_computation.17 | loop fusion | flops 1540096 | bytes 1054720 | tf_op jit(solution)/shard_map/reduce_sum | solution.py:62
  5.5 1.4 %fusion.20 = (bf16[64,256]{1,0:T(8,128)(2,1)S(1)}, bf16[64,256]{1,0:T(8,128)(2,1)}) fusion(f32[64,256]{1,0:T(8,128)S(1)} %get-tuple-element.12, f32[256]{0:T(256)S(1)} %bitcast.64, s32[256]{0:T(256)} %bitcast.66, s32[64]{0:T(128)S(1)} %iota_add_fusion, f32[64,256]{1,0:T(8,128)S(1)} %get-tuple-element.13, f32[256]{0:T(256)S(1)} %bitcast.65), kind=kLoop, calls=%fused_computation.31 | loop fusion | flops 114688 | bytes 199936 | tf_op jit(solution)/shard_map/convert_element_type | solution.py:67
  6.9 20.0 %all_gather.6 = bf16[1024,256]{1,0:T(8,128)(2,1)S(1)} all-gather(bf16[64,256]{1,0:T(8,128)(2,1)S(1)} %get-tuple-element.18), channel_id=1, replica_groups=mesh['sub'=32,'blk'=16] {'blk'}, dimensions={0}, use_global_device_ids=true | all-gather | bytes 557056 | tf_op jit(solution)/shard_map/all_gather | solution.py:73
  26.9 0.8 fusion.4
  27.7 1.3 %copy.22 = f32[1024,256]{1,0:T(8,128)} copy(f32[1024,256]{0,1:T(8,128)S(1)} %fusion.4) | data formatting | bytes 2097152 | tf_op jit(solution)/shard_map/dot_general | solution.py:71
  29.0 0.6 pad_clamp_fusion.1
  29.6 0.2 convert_reduce_fusion
  29.8 0.6 fusion.30
  30.3 0.5 multiply_bitcast_fusion
  30.9 2.2 %scatter_custom_fusion = f32[192,256]{1,0:T(8,128)S(1)} fusion(s32[64]{0:T(128)} %fusion.30, f32[]{:T(128)} %constant.11.clone.1, f32[64,256]{1,0:T(8,128)S(1)} %get-tuple-element.12, f32[64]{0:T(128)} %multiply_bitcast_fusion, f32[1024,256]{1,0:T(8,128)} %copy.22, s32[1024]{0:T(1024)} %pad_clamp_fusion.1), kind=kCustom, calls=%fused_computation.26 | custom fusion | flops 32768 | bytes 1315840 | tf_op jit(solution)/shard_map/scatter | solution.py:24
  33.0 0.7 reshape.153
  33.8 21.0 %all-to-all-start = ((f32[32,6,256]{2,1,0:T(8,128)}), f32[32,6,256]{2,1,0:T(8,128)S(1)}, u32[]{:S(2)}, u32[]{:S(2)}) async-start(f32[32,6,256]{2,1,0:T(8,128)} %reshape.153), calls=%async_computation | async-start | bytes 524288 | tf_op jit(solution)/shard_map/all_to_all | solution.py:25
  54.8 19.7 %all_gather.7 = bf16[1024,256]{1,0:T(8,128)(2,1)S(1)} all-gather(bf16[64,256]{1,0:T(8,128)(2,1)} %get-tuple-element.19), channel_id=1, replica_groups=mesh['sub'=32,'blk'=16] {'blk'}, dimensions={0}, use_global_device_ids=true | all-gather | bytes 557056 | tf_op jit(solution)/shard_map/all_gather | solution.py:73
  74.5 1.8 %fusion.7 = f32[1024,256]{0,1:T(8,128)} fusion(bf16[1024,256]{1,0:T(8,128)(2,1)S(1)} %all_gather.7, bf16[1,1024,1024]{2,1,0:T(8,128)(2,1)S(1)} %copy-done), kind=kOutput, calls=%fused_computation.11 | convolution fusion | flops 536870912 | bytes 3670016 | tf_op jit(solution)/shard_map/dot_general | solution.py:71
  76.3 2.6 %copy.23 = f32[1024,256]{1,0:T(8,128)} copy(f32[1024,256]{0,1:T(8,128)} %fusion.7) | data formatting | bytes 2097152 | tf_op jit(solution)/shard_map/dot_general | solution.py:71
  78.9 2.8 %scatter_custom_fusion.1 = f32[192,256]{1,0:T(8,128)} fusion(s32[64]{0:T(128)} %fusion.30, f32[]{:T(128)} %constant.11.clone.1, f32[64,256]{1,0:T(8,128)S(1)} %get-tuple-element.13, f32[64]{0:T(128)} %multiply_bitcast_fusion, f32[1024,256]{1,0:T(8,128)} %copy.23, s32[1024]{0:T(1024)} %pad_clamp_fusion.1), kind=kCustom, calls=%fused_computation.24 | custom fusion | flops 32768 | bytes 1315840 | tf_op jit(solution)/shard_map/scatter | solution.py:24
  81.6 1.7 %reshape.155 = f32[32,6,256]{2,1,0:T(8,128)} reshape(f32[192,256]{1,0:T(8,128)} %scatter_custom_fusion.1) | data formatting | bytes 393216 | tf_op jit(solution)/shard_map/reshape | solution.py:26
  83.3 16.0 %all-to-all-start.1 = ((f32[32,6,256]{2,1,0:T(8,128)}), f32[32,6,256]{2,1,0:T(8,128)}, u32[]{:S(2)}, u32[]{:S(2)}) async-start(f32[32,6,256]{2,1,0:T(8,128)} %reshape.155), calls=%async_computation.1 | async-start | bytes 524288 | tf_op jit(solution)/shard_map/all_to_all | solution.py:25
  99.3 2.2 %fusion.12 = bf16[1,1024,256]{1,2,0:T(8,128)(2,1)} fusion(f32[1024,256]{0,1:T(8,128)} %fusion.7, f32[1024,256]{0,1:T(8,128)S(1)} %fusion.4), kind=kLoop, calls=%fused_computation.18 | loop fusion | flops 1310720 | bytes 2621440 | tf_op jit(solution)/shard_map/broadcast_in_dim | solution.py:83
  101.5 2.0 %copy.24 = bf16[1,1024,256]{2,1,0:T(8,128)(2,1)} copy(bf16[1,1024,256]{1,2,0:T(8,128)(2,1)} %fusion.12) | data formatting | bytes 1048576
  103.6 0.6 pad_clamp_fusion
  104.2 2.3 %multiply_add_fusion = f32[1,12,64,256]{3,2,1,0:T(8,128)} fusion(f32[1,12,64,256]{3,2,1,0:T(8,128)} %param.18, f32[64,256]{1,0:T(8,128)S(1)} %copy-done.2, f32[64,256]{1,0:T(8,128)S(1)} %get-tuple-element.14, f32[12,64]{1,0:T(8,128)S(1)} %get-tuple-element.24, f32[12,64]{1,0:T(8,128)S(1)} %get-tuple-element.25), kind=kLoop, calls=%fused_computation.15 | loop fusion | flops 1179648 | bytes 1710080 | tf_op jit(solution)/shard_map/add | solution.py:61
  106.5 0.7 gather_fusion
  107.2 14.1 %all-to-all-done.1 = f32[32,6,256]{2,1,0:T(8,128)} async-done(((f32[32,6,256]{2,1,0:T(8,128)}), f32[32,6,256]{2,1,0:T(8,128)}, u32[]{:S(2)}, u32[]{:S(2)}) %all-to-all-start.1) | async-done | bytes 196640 | tf_op jit(solution)/shard_map/all_to_all | solution.py:25
  121.3 1.0 reshape.156
  122.3 0.7 gather_fusion.1
  123.0 0.8 copy.25
  (17 shorter events, 0.1 us)
Async XLA Ops:
  0.6 26.2 %copy-start = (bf16[1,1024,1024]{2,1,0:T(8,128)(2,1)S(1)}, bf16[1,1024,1024]{2,1,0:T(8,128)(2,1)}, u32[]{:S(2)}) copy-start(bf16[1,1024,1024]{2,1,0:T(8,128)(2,1)} %param.11) | copy-start | bytes 6291460
  4.0 2.8 %copy-start.1 = (f32[64,256]{1,0:T(8,128)}, f32[64,256]{1,0:T(8,128)S(1)}, u32[]{:S(2)}) copy-start(f32[64,256]{1,0:T(8,128)S(1)} %get-tuple-element.15) | copy-start | bytes 196612
  26.9 2.1 %copy-start.3 = (s32[1,64]{1,0:T(1,128)S(1)}, s32[1,64]{1,0:T(1,128)}, u32[]{:S(2)}) copy-start(s32[1,64]{1,0:T(1,128)} %param.12) | copy-start | bytes 772
  26.9 2.7 %copy-start.4 = (s32[1,64]{1,0:T(1,128)S(1)}, s32[1,64]{1,0:T(1,128)}, u32[]{:S(2)}) copy-start(s32[1,64]{1,0:T(1,128)} %param.13) | copy-start | bytes 772
  26.9 3.5 %copy-start.5 = (f32[1,64]{1,0:T(1,128)S(1)}, f32[1,64]{1,0:T(1,128)}, u32[]{:S(2)}) copy-start(f32[1,64]{1,0:T(1,128)} %param.15) | copy-start | bytes 772
  33.8 49.5 %all-to-all-start = ((f32[32,6,256]{2,1,0:T(8,128)}), f32[32,6,256]{2,1,0:T(8,128)S(1)}, u32[]{:S(2)}, u32[]{:S(2)}) async-start(f32[32,6,256]{2,1,0:T(8,128)} %reshape.153), calls=%async_computation | async-start | bytes 524288 | tf_op jit(solution)/shard_map/all_to_all | solution.py:25
  83.3 20.9 %copy-start.2 = (f32[64,256]{1,0:T(8,128)S(1)}, f32[64,256]{1,0:T(8,128)}, u32[]{:S(2)}) copy-start(f32[64,256]{1,0:T(8,128)} %copy-done.1) | copy-start | bytes 196612
  83.3 38.0 %all-to-all-start.1 = ((f32[32,6,256]{2,1,0:T(8,128)}), f32[32,6,256]{2,1,0:T(8,128)}, u32[]{:S(2)}, u32[]{:S(2)}) async-start(f32[32,6,256]{2,1,0:T(8,128)} %reshape.155), calls=%async_computation.1 | async-start | bytes 524288 | tf_op jit(solution)/shard_map/all_to_all | solution.py:25
where the time goes:
time: 125 us; the launch traced here: 124 us
  blocking collectives  39.7 us (32%)
  starting transfers between devices  37 us (30%)
  other arithmetic  16.7 us (13%)
  waiting for transfers between devices  14.1 us (11%)
  local copies, waits for them, and re-layouts  12.9 us (10%)
  matrix products  2.53 us (2%)
    all_gather x2, blocking collectives, body(): lax.all_gather(injections[step_index], 'blk', axis=0, tiled=True)  39.7 us
    all_to_all x2, starting transfers between devices, deliver(): lax.all_to_all(outbox.reshape(systems, capacity, columns), 'sub', split_a...  37 us
    all_to_all x2, waiting for transfers between devices, deliver(): lax.all_to_all(outbox.reshape(systems, capacity, columns), 'sub', split_a...  14.1 us
    scatter x2, other arithmetic, deliver(): jnp.zeros((systems * capacity, columns), jnp.float32).at[slot_rows]  4.9 us
    dot_general x2, local copies, waits for them, and re-layouts, body(): jnp.dot(matrix, lax.all_gather(injections[step_index], 'blk', axis=0, til...  3.92 us
    unnamed x15, local copies, waits for them, and re-layouts  3.55 us
    dot_general x2, matrix products, body(): jnp.dot(matrix, lax.all_gather(injections[step_index], 'blk', axis=0, til...  2.53 us
  transfers between devices with their start and end apart: 2, of which 1 were waited for; matrix products, arithmetic and copies ran while one was open for 13% of the time, Pallas kernels for 0%

commit v1 on v0

--- a/solution.py
+++ b/solution.py
@@ -1,7 +1,21 @@
+import functools
 import jax
 import jax.numpy as jnp
 from jax import lax
 from jax.sharding import PartitionSpec as P
+
+
+def node_fill(xx, which_axis):
+    e_now = jnp.concatenate(
+        lax.all_to_all(
+            jnp.stack([xx for _ in range(lax.psum(1, axis_name=which_axis))], 0), which_axis, 0, 0
+        ),
+        0,
+    )
+    return e_now
+
+
+obtain_the_loops = functools.partial(node_fill, which_axis="blk")
 
 
 def pick_incident(history, delays, step_index):
@@ -69,9 +83,7 @@
     arrivals = []
     for step_index in range(steps_total):
         voltage = jnp.dot(
-            matrix,
-            lax.all_gather(injections[step_index], "blk", axis=0, tiled=True),
-            preferred_element_type=jnp.float32,
+            matrix, obtain_the_loops(injections[step_index]), preferred_element_type=jnp.float32
         )
         voltages.append(voltage)
         emitted_now = 2.0 * line_admittance * voltage[local_nodes] - sources[step_index]

time: 125 us -> 111 us (0.89)
  blocking collectives: 39.7 us -> 0 us
  waiting for transfers between devices: 14.1 us -> 37.9 us
  local copies, waits for them, and re-layouts: 12.9 us -> 15.3 us
  matrix products: 2.53 us -> 4.56 us
  other arithmetic: 16.7 us -> 14.9 us
    all_gather x2 -> x0, blocking collectives: 39.7 us -> none  [body(): lax.all_gather(injections[step_index], 'blk', axis=0, tiled=True)]
    all_to_all x2, waiting for transfers between devices: 14.1 us -> 27.5 us  [deliver(): lax.all_to_all(outbox.reshape(systems, capacity, columns), 'sub', split_a...]
    all_to_all x0 -> x2, starting transfers between devices: none -> 11.8 us  [node_fill(): lax.all_to_all(jnp.stack([xx for _ in range(lax.psum(1, axis_name=which_a...]
    all_to_all x2, starting transfers between devices: 37 us -> 25.3 us  [deliver(): lax.all_to_all(outbox.reshape(systems, capacity, columns), 'sub', split_a...]
    all_to_all x0 -> x2, waiting for transfers between devices: none -> 10.3 us  [node_fill(): lax.all_to_all(jnp.stack([xx for _ in range(lax.psum(1, axis_name=which_a...]
    dot_general x2, matrix products: 2.53 us -> 4.56 us  [body(): jnp.dot(matrix, obtain_the_loops(injections[step_index]), preferred_eleme...]
    another operation x0 -> x2, local copies, waits for them, and re-layouts: none -> 1.74 us  [node_fill(): jnp.stack([xx for _ in range(lax.psum(1, axis_name=which_axis))], 0)]
    unnamed x15 -> x17, local copies, waits for them, and re-layouts: 3.55 us -> 4.16 us
  transfers between devices with their start and end apart: 2 -> 4, of which waited for: 1 -> 4; matrix products, arithmetic and copies ran while one was open for 13% -> 22% of each run, Pallas kernels for 0% -> 0%
where the time goes in v1:
time: 111 us; the launch traced here: 110 us
  waiting for transfers between devices  37.9 us (34%)
  starting transfers between devices  37.1 us (33%)
  local copies, waits for them, and re-layouts  15.3 us (14%)
  other arithmetic  14.9 us (13%)
  matrix products  4.56 us (4%)
    all_to_all x2, waiting for transfers between devices, deliver(): lax.all_to_all(outbox.reshape(systems, capacity, columns), 'sub', split_a...  27.5 us
    all_to_all x2, starting transfers between devices, deliver(): lax.all_to_all(outbox.reshape(systems, capacity, columns), 'sub', split_a...  25.3 us
    all_to_all x2, starting transfers between devices, node_fill(): lax.all_to_all(jnp.stack([xx for _ in range(lax.psum(1, axis_name=which_a...  11.8 us
    all_to_all x2, waiting for transfers between devices, node_fill(): lax.all_to_all(jnp.stack([xx for _ in range(lax.psum(1, axis_name=which_a...  10.3 us
    scatter x2, other arithmetic, deliver(): jnp.zeros((systems * capacity, columns), jnp.float32).at[slot_rows]  4.92 us
    dot_general x2, matrix products, body(): jnp.dot(matrix, obtain_the_loops(injections[step_index]), preferred_eleme...  4.56 us
    unnamed x17, local copies, waits for them, and re-layouts  4.16 us
    dot_general x2, local copies, waits for them, and re-layouts, body(): jnp.dot(matrix, obtain_the_loops(injections[step_index]), preferred_eleme...  3.88 us
  transfers between devices with their start and end apart: 4, of which 4 were waited for; matrix products, arithmetic and copies ran while one was open for 22% of the time, Pallas kernels for 0%

profile of v1, /device:TPU:1, one launch (start us, length us, event | category | flops | bytes accessed | tf_op | source)
XLA Modules:
  0.0 110.4 jit_solution(17903432958933525136)
XLA Ops:
  0.7 0.8 add_bitcast_fusion
  1.5 0.8 fusion.34
  2.2 0.7 copy_bitcast_fusion
  3.0 1.1 fusion.13
  4.7 1.4 %fusion.11 = (f32[64,256]{1,0:T(8,128)S(1)}, f32[64,256]{1,0:T(8,128)S(1)}) fusion(f32[1,12,64,256]{3,2,1,0:T(8,128)} %param.18, f32[64,256]{1,0:T(8,128)S(1)} %get-tuple-element.14, f32[12,64]{1,0:T(8,128)S(1)} %get-tuple-element.24, f32[12,64]{1,0:T(8,128)S(1)} %get-tuple-element.25, f32[64,256]{1,0:T(8,128)S(1)} %get-tuple-element.15), kind=kLoop, calls=%fused_computation.17 | loop fusion | flops 1540096 | bytes 1054720 | tf_op jit(solution)/shard_map/reduce_sum | solution.py:76
  6.1 0.8 fusion.20
  6.9 0.8 stack.10
  7.7 7.6 %all-to-all-start = ((bf16[16,64,256]{2,1,0:T(8,128)(2,1)}), bf16[16,64,256]{2,1,0:T(8,128)(2,1)S(1)}, u32[]{:S(2)}, u32[]{:S(2)}) async-start(bf16[16,64,256]{2,1,0:T(8,128)(2,1)} %stack.10), calls=%async_computation | async-start | bytes 1048576 | tf_op jit(solution)/shard_map/all_to_all | solution.py:10
  16.7 7.7 %all-to-all-done = bf16[16,64,256]{2,1,0:T(8,128)(2,1)S(1)} async-done(((bf16[16,64,256]{2,1,0:T(8,128)(2,1)}), bf16[16,64,256]{2,1,0:T(8,128)(2,1)S(1)}, u32[]{:S(2)}, u32[]{:S(2)}) %all-to-all-start) | async-done | bytes 524320 | tf_op jit(solution)/shard_map/all_to_all | solution.py:10
  24.3 0.9 stack.11
  25.2 4.2 %all-to-all-start.1 = ((bf16[16,64,256]{2,1,0:T(8,128)(2,1)}), bf16[16,64,256]{2,1,0:T(8,128)(2,1)}, u32[]{:S(2)}, u32[]{:S(2)}) async-start(bf16[16,64,256]{2,1,0:T(8,128)(2,1)} %stack.11), calls=%async_computation.1 | async-start | bytes 1048576 | tf_op jit(solution)/shard_map/all_to_all | solution.py:10
  30.0 1.8 %fusion.4 = f32[1024,256]{0,1:T(8,128)S(1)} fusion(bf16[1024,256]{1,0:T(8,128)(2,1)} %bitcast.64, bf16[1,1024,1024]{2,1,0:T(8,128)(2,1)S(1)} %copy-done), kind=kOutput, calls=%fused_computation.10 | convolution fusion | flops 536870912 | bytes 3670016 | tf_op jit(solution)/shard_map/dot_general | solution.py:85
  31.8 1.3 %copy.22 = f32[1024,256]{1,0:T(8,128)} copy(f32[1024,256]{0,1:T(8,128)S(1)} %fusion.4) | data formatting | bytes 2097152 | tf_op jit(solution)/shard_map/dot_general | solution.py:85
  33.1 2.2 %scatter_custom_fusion = f32[192,256]{1,0:T(8,128)S(1)} fusion(s32[64]{0:T(128)} %fusion.30, f32[]{:T(128)} %constant.11.clone.1, f32[64,256]{1,0:T(8,128)S(1)} %get-tuple-element.12, f32[64]{0:T(128)} %multiply_bitcast_fusion, f32[1024,256]{1,0:T(8,128)} %copy.22, s32[1024]{0:T(1024)} %pad_clamp_fusion.1), kind=kCustom, calls=%fused_computation.26 | custom fusion | flops 32768 | bytes 1315840 | tf_op jit(solution)/shard_map/scatter | solution.py:38
  35.3 0.7 reshape.219
  36.0 2.7 %all-to-all-done.1 = bf16[16,64,256]{2,1,0:T(8,128)(2,1)} async-done(((bf16[16,64,256]{2,1,0:T(8,128)(2,1)}), bf16[16,64,256]{2,1,0:T(8,128)(2,1)}, u32[]{:S(2)}, u32[]{:S(2)}) %all-to-all-start.1) | async-done | bytes 524320 | tf_op jit(solution)/shard_map/all_to_all | solution.py:10
  38.7 20.1 %all-to-all-start.2 = ((f32[32,6,256]{2,1,0:T(8,128)}), f32[32,6,256]{2,1,0:T(8,128)S(1)}, u32[]{:S(2)}, u32[]{:S(2)}) async-start(f32[32,6,256]{2,1,0:T(8,128)} %reshape.219), calls=%async_computation.2 | async-start | bytes 524288 | tf_op jit(solution)/shard_map/all_to_all | solution.py:39
  58.8 2.8 %fusion.7 = f32[1024,256]{0,1:T(8,128)} fusion(bf16[1024,256]{1,0:T(8,128)(2,1)} %bitcast.10, bf16[1,1024,1024]{2,1,0:T(8,128)(2,1)S(1)} %copy-done), kind=kOutput, calls=%fused_computation.11 | convolution fusion | flops 536870912 | bytes 3670016 | tf_op jit(solution)/shard_map/dot_general | solution.py:85
  61.5 2.6 %copy.23 = f32[1024,256]{1,0:T(8,128)} copy(f32[1024,256]{0,1:T(8,128)} %fusion.7) | data formatting | bytes 2097152 | tf_op jit(solution)/shard_map/dot_general | solution.py:85
  64.1 2.8 %scatter_custom_fusion.1 = f32[192,256]{1,0:T(8,128)} fusion(s32[64]{0:T(128)} %fusion.30, f32[]{:T(128)} %constant.11.clone.1, f32[64,256]{1,0:T(8,128)S(1)} %get-tuple-element.13, f32[64]{0:T(128)} %multiply_bitcast_fusion, f32[1024,256]{1,0:T(8,128)} %copy.23, s32[1024]{0:T(1024)} %pad_clamp_fusion.1), kind=kCustom, calls=%fused_computation.24 | custom fusion | flops 32768 | bytes 1315840 | tf_op jit(solution)/shard_map/scatter | solution.py:38
  66.9 1.7 %reshape.221 = f32[32,6,256]{2,1,0:T(8,128)} reshape(f32[192,256]{1,0:T(8,128)} %scatter_custom_fusion.1) | data formatting | bytes 393216 | tf_op jit(solution)/shard_map/reshape | solution.py:40
  68.5 12.2 %all-to-all-done.2 = f32[32,6,256]{2,1,0:T(8,128)S(1)} async-done(((f32[32,6,256]{2,1,0:T(8,128)}), f32[32,6,256]{2,1,0:T(8,128)S(1)}, u32[]{:S(2)}, u32[]{:S(2)}) %all-to-all-start.2) | async-done | bytes 196640 | tf_op jit(solution)/shard_map/all_to_all | solution.py:39
  80.8 5.2 %all-to-all-start.3 = ((f32[32,6,256]{2,1,0:T(8,128)}), f32[32,6,256]{2,1,0:T(8,128)}, u32[]{:S(2)}, u32[]{:S(2)}) async-start(f32[32,6,256]{2,1,0:T(8,128)} %reshape.221), calls=%async_computation.3 | async-start | bytes 524288 | tf_op jit(solution)/shard_map/all_to_all | solution.py:39
  86.0 0.7 pad_clamp_fusion
  86.7 2.3 %multiply_add_fusion = f32[1,12,64,256]{3,2,1,0:T(8,128)} fusion(f32[1,12,64,256]{3,2,1,0:T(8,128)} %param.18, f32[64,256]{1,0:T(8,128)} %copy-done.3, f32[64,256]{1,0:T(8,128)S(1)} %get-tuple-element.14, f32[12,64]{1,0:T(8,128)S(1)} %get-tuple-element.24, f32[12,64]{1,0:T(8,128)S(1)} %get-tuple-element.25), kind=kLoop, calls=%fused_computation.15 | loop fusion | flops 1179648 | bytes 1710080 | tf_op jit(solution)/shard_map/add | solution.py:75
  89.0 1.0 fusion.12
  90.0 2.0 %copy.24 = bf16[1,1024,256]{2,1,0:T(8,128)(2,1)} copy(bf16[1,1024,256]{1,2,0:T(8,128)(2,1)} %fusion.12) | data formatting | bytes 1048576
  92.1 0.7 gather_fusion
  92.7 15.3 %all-to-all-done.3 = f32[32,6,256]{2,1,0:T(8,128)} async-done(((f32[32,6,256]{2,1,0:T(8,128)}), f32[32,6,256]{2,1,0:T(8,128)}, u32[]{:S(2)}, u32[]{:S(2)}) %all-to-all-start.3) | async-done | bytes 196640 | tf_op jit(solution)/shard_map/all_to_all | solution.py:39
  108.0 1.0 reshape.222
  109.0 0.7 gather_fusion.1
  109.7 0.8 copy.25
  (23 shorter events, 2.5 us)
Async XLA Ops:
  0.6 29.4 %copy-start = (bf16[1,1024,1024]{2,1,0:T(8,128)(2,1)S(1)}, bf16[1,1024,1024]{2,1,0:T(8,128)(2,1)}, u32[]{:S(2)}) copy-start(bf16[1,1024,1024]{2,1,0:T(8,128)(2,1)} %param.11) | copy-start | bytes 6291460
  0.6 14.7 %copy-start.4 = (s32[1,64]{1,0:T(1,128)S(1)}, s32[1,64]{1,0:T(1,128)}, u32[]{:S(2)}) copy-start(s32[1,64]{1,0:T(1,128)} %param.12) | copy-start | bytes 772
  0.7 15.3 %copy-start.5 = (s32[1,64]{1,0:T(1,128)S(1)}, s32[1,64]{1,0:T(1,128)}, u32[]{:S(2)}) copy-start(s32[1,64]{1,0:T(1,128)} %param.13) | copy-start | bytes 772
  4.1 0.6 copy-start.3
  4.7 24.8 %copy-start.6 = (f32[1,64]{1,0:T(1,128)S(1)}, f32[1,64]{1,0:T(1,128)}, u32[]{:S(2)}) copy-start(f32[1,64]{1,0:T(1,128)} %param.15) | copy-start | bytes 772
  7.7 16.6 %all-to-all-start = ((bf16[16,64,256]{2,1,0:T(8,128)(2,1)}), bf16[16,64,256]{2,1,0:T(8,128)(2,1)S(1)}, u32[]{:S(2)}, u32[]{:S(2)}) async-start(bf16[16,64,256]{2,1,0:T(8,128)(2,1)} %stack.10), calls=%async_computation | async-start | bytes 1048576 | tf_op jit(solution)/shard_map/all_to_all | solution.py:10
  24.3 5.7 %copy-start.2 = (bf16[16,64,256]{2,1,0:T(8,128)(2,1)}, bf16[16,64,256]{2,1,0:T(8,128)(2,1)S(1)}, u32[]{:S(2)}) copy-start(bf16[16,64,256]{2,1,0:T(8,128)(2,1)S(1)} %all-to-all-done) | copy-start | bytes 1572868
  25.2 13.5 %all-to-all-start.1 = ((bf16[16,64,256]{2,1,0:T(8,128)(2,1)}), bf16[16,64,256]{2,1,0:T(8,128)(2,1)}, u32[]{:S(2)}, u32[]{:S(2)}) async-start(bf16[16,64,256]{2,1,0:T(8,128)(2,1)} %stack.11), calls=%async_computation.1 | async-start | bytes 1048576 | tf_op jit(solution)/shard_map/all_to_all | solution.py:10
  38.7 42.1 %all-to-all-start.2 = ((f32[32,6,256]{2,1,0:T(8,128)}), f32[32,6,256]{2,1,0:T(8,128)S(1)}, u32[]{:S(2)}, u32[]{:S(2)}) async-start(f32[32,6,256]{2,1,0:T(8,128)} %reshape.219), calls=%async_computation.2 | async-start | bytes 524288 | tf_op jit(solution)/shard_map/all_to_all | solution.py:39
  80.8 27.2 %all-to-all-start.3 = ((f32[32,6,256]{2,1,0:T(8,128)}), f32[32,6,256]{2,1,0:T(8,128)}, u32[]{:S(2)}, u32[]{:S(2)}) async-start(f32[32,6,256]{2,1,0:T(8,128)} %reshape.221), calls=%async_computation.3 | async-start | bytes 524288 | tf_op jit(solution)/shard_map/all_to_all | solution.py:39
  86.0 3.0 %copy-start.1 = (f32[1024,256]{0,1:T(8,128)S(1)}, f32[1024,256]{0,1:T(8,128)}, u32[]{:S(2)}) copy-start(f32[1024,256]{0,1:T(8,128)} %fusion.7) | copy-start | bytes 3145732
